TPU v7x, 32 devices: a whole 2x2x4 slice. The times are simulated.
32 devices in a mesh: blk: 8 (over z, y), rank: 4 (over x, core).
Axes of the slice: x: 2, y: 2, z: 4, core: 2. Of those that a mesh axis runs over, the one named last changes fastest.
Arguments:
- user_factors: float32 [256, 4096], P('rank', 'blk'), may hold values from -1.5 to 1.5
- item_factors: float32 [256, 8192], P('rank', 'blk'), may hold values from -1.5 to 1.5
- tile_rows: int32 [8, 4, 4096], P('blk'), may hold values from 0 to 511
- tile_cols: int32 [8, 4, 4096], P('blk'), may hold values from 0 to 1023
- tile_vals: float32 [8, 4, 4096], P('blk'), may hold values from -4 to 4
- tile_count: int32 [8, 4], P('blk'), may hold values from 512 to 4096, as said below
Outputs:
- new_users: float32 [256, 4096], P('rank', 'blk')
- new_items: float32 [256, 8192], P('rank', 'blk')
Inputs may be any that keep to these rules, and one draw needn't show every extreme that they name: `tile_count`: in every stratum some block's tile is full (4096 live slots).
All inputs are finite; a program needn't handle non-finite values.
Results may differ from a plain program's by a relative error of at most 0.0003.
Values sent between devices are 32-bit elements; how exact they have to be, the bound alone decides.
A program may use at most 64 MiB of HBM per device.

v0:
```python
import jax
import jax.numpy as jnp
from jax import lax
from jax.sharding import PartitionSpec as P

BATCH = 1024
STRATA = 4
LEARN_RATE = 0.05
DECAY_WEIGHT = 0.02


def shifted(block, axis, distance):
    devices = range(lax.axis_size(axis))
    route = [((i - distance) % len(devices), i) for i in devices]
    return lax.ppermute(block, axis, route)


def rank_total(partial_values):
    return lax.psum(partial_values, "rank")


def selector(indices, count):
    places = jnp.arange(count, dtype=jnp.int32)[:, None]
    return (places == indices[None, :]).astype(jnp.float32)


def pick_columns(block, chooser):
    return jnp.dot(
        block, chooser, preferred_element_type=jnp.float32, precision=lax.Precision.HIGHEST
    )


def spread_columns(steps, chooser):
    return lax.dot_general(
        steps,
        chooser,
        (((1,), (1,)), ((), ())),
        preferred_element_type=jnp.float32,
        precision=lax.Precision.HIGHEST,
    )


def sweep_tile(user_block, item_block, row_index, col_index, rating_vals, live_count, combiner):
    user_count = user_block.shape[1]
    item_count = item_block.shape[1]

    def update(batch_index, carry):
        user_now, item_now = carry
        offset = (batch_index * BATCH).astype(jnp.int32)
        user_rows = lax.dynamic_slice_in_dim(row_index, offset, BATCH)
        item_rows = lax.dynamic_slice_in_dim(col_index, offset, BATCH)
        targets = lax.dynamic_slice_in_dim(rating_vals, offset, BATCH)
        positions = offset + jnp.arange(BATCH, dtype=jnp.int32)
        weights = (positions < live_count).astype(jnp.float32)
        user_pick = selector(user_rows, user_count)
        item_pick = selector(item_rows, item_count)
        user_vecs = pick_columns(user_now, user_pick)
        item_vecs = pick_columns(item_now, item_pick)
        predicted = combiner(jnp.sum(user_vecs * item_vecs, axis=0))
        errors = weights * (targets - predicted)
        user_step = LEARN_RATE * (
            errors[None, :] * item_vecs - DECAY_WEIGHT * weights[None, :] * user_vecs
        )
        item_step = LEARN_RATE * (
            errors[None, :] * user_vecs - DECAY_WEIGHT * weights[None, :] * item_vecs
        )
        return (
            user_now + spread_columns(user_step, user_pick),
            item_now + spread_columns(item_step, item_pick),
        )

    return lax.fori_loop(0, row_index.shape[0] // BATCH, update, (user_block, item_block))


def per_device(user_factors, item_factors, tile_rows, tile_cols, tile_vals, tile_count):
    user_block = user_factors
    item_block = item_factors
    for stratum in range(STRATA):
        if stratum > 0:
            item_block = shifted(item_block, "blk", 1)
        user_block, item_block = sweep_tile(
            user_block,
            item_block,
            tile_rows[0, stratum],
            tile_cols[0, stratum],
            tile_vals[0, stratum],
            tile_count[0, stratum],
            rank_total,
        )
    item_block = shifted(item_block, "blk", 1 - STRATA)
    return (user_block, item_block)


def solution(mesh):
    placed = (
        P("rank", "blk"),
        P("rank", "blk"),
        P("blk", None, None),
        P("blk", None, None),
        P("blk", None, None),
        P("blk", None),
    )
    return jax.shard_map(
        per_device,
        mesh=mesh,
        in_specs=placed,
        out_specs=(P("rank", "blk"), P("rank", "blk")),
        check_vma=False,
    )
```

profile of v0, /device:TPU:28, one launch (start us, length us, event | category | flops | bytes accessed | tf_op | source)
XLA Modules:
  0.0 258.6 jit_solution(12740042411596117091)
XLA Ops:
  2.2 53.7 %while.60 = (s32[]{:T(128)}, f32[64,512]{1,0:T(8,128)S(1)}, f32[64,1024]{1,0:T(8,128)S(1)}, s32[]{:T(128)}, f32[4096]{0:T(1024)S(1)}, /*index=5*/s32[4096]{0:T(1...) while((s32[]{:T(128)}, f32[64,512]{1,0:T(8,128)S(1)}, ...), condition=%wide.region_3.0_spmd, body=%wide.region_0.0_spmd.sunk | while | flops 2419825664 | bytes 3092663 | solution.py:72
  5.4 6.9 %psum.48 = f32[1024]{0:T(1024)S(1)} all-reduce(f32[1024]{0:T(1024)S(1)} %get-tuple-element.750), channel_id=1, replica_groups=mesh['blk'=8,'rank'=4] {'rank'}, use_global_device_ids=true, to_apply=%region_2.0 | all-reduce | flops 1024 | bytes 8192 | tf_op jit(solution)/shard_map/while/body/eval_jaxpr/psum | solution.py:19
  14.1 2.3 fusion.159
  19.6 5.9 %psum.48 = f32[1024]{0:T(1024)S(1)} all-reduce(f32[1024]{0:T(1024)S(1)} %get-tuple-element.750), channel_id=1, replica_groups=mesh['blk'=8,'rank'=4] {'rank'}, use_global_device_ids=true, to_apply=%region_2.0 | all-reduce | flops 1024 | bytes 8192 | tf_op jit(solution)/shard_map/while/body/eval_jaxpr/psum | solution.py:19
  27.4 2.3 fusion.159
  32.9 5.8 %psum.48 = f32[1024]{0:T(1024)S(1)} all-reduce(f32[1024]{0:T(1024)S(1)} %get-tuple-element.750), channel_id=1, replica_groups=mesh['blk'=8,'rank'=4] {'rank'}, use_global_device_ids=true, to_apply=%region_2.0 | all-reduce | flops 1024 | bytes 8192 | tf_op jit(solution)/shard_map/while/body/eval_jaxpr/psum | solution.py:19
  40.5 2.3 fusion.159
  46.0 5.7 %psum.48 = f32[1024]{0:T(1024)S(1)} all-reduce(f32[1024]{0:T(1024)S(1)} %get-tuple-element.750), channel_id=1, replica_groups=mesh['blk'=8,'rank'=4] {'rank'}, use_global_device_ids=true, to_apply=%region_2.0 | all-reduce | flops 1024 | bytes 8192 | tf_op jit(solution)/shard_map/while/body/eval_jaxpr/psum | solution.py:19
  53.6 2.3 fusion.159
  56.0 8.0 %collective-permute-done = f32[64,1024]{1,0:T(8,128)S(1)} collective-permute-done((f32[64,1024]{1,0:T(8,128)S(1)}, f32[64,1024]{1,0:T(8,128)S(1)}, u32[]{:S(2)}, u32[]{:S(2)}) %collective-permute-start) | collective-permute-done | bytes 262176 | tf_op jit(solution)/shard_map/ppermute | solution.py:15
  64.0 53.0 %while.61 = (s32[]{:T(128)}, f32[64,512]{1,0:T(8,128)S(1)}, f32[64,1024]{1,0:T(8,128)S(1)}, s32[]{:T(128)}, f32[4096]{0:T(1024)S(1)}, /*index=5*/s32[4096]{0:T(1...) while((s32[]{:T(128)}, f32[64,512]{1,0:T(8,128)S(1)}, ...), condition=%wide.region_7.0_spmd, body=%wide.region_4.0_spmd.sunk | while | flops 2419825664 | bytes 3092663 | solution.py:72
  67.1 5.7 %psum.49 = f32[1024]{0:T(1024)S(1)} all-reduce(f32[1024]{0:T(1024)S(1)} %get-tuple-element.759), channel_id=1, replica_groups=mesh['blk'=8,'rank'=4] {'rank'}, use_global_device_ids=true, to_apply=%region_6.0 | all-reduce | flops 1024 | bytes 8192 | tf_op jit(solution)/shard_map/while/body/eval_jaxpr/psum | solution.py:19
  74.5 2.3 fusion.167
  77.5 1.6 fusion.164
  80.0 6.6 %psum.49 = f32[1024]{0:T(1024)S(1)} all-reduce(f32[1024]{0:T(1024)S(1)} %get-tuple-element.759), channel_id=1, replica_groups=mesh['blk'=8,'rank'=4] {'rank'}, use_global_device_ids=true, to_apply=%region_6.0 | all-reduce | flops 1024 | bytes 8192 | tf_op jit(solution)/shard_map/while/body/eval_jaxpr/psum | solution.py:19
  88.3 2.3 fusion.167
  91.3 1.6 fusion.164
  93.8 5.7 %psum.49 = f32[1024]{0:T(1024)S(1)} all-reduce(f32[1024]{0:T(1024)S(1)} %get-tuple-element.759), channel_id=1, replica_groups=mesh['blk'=8,'rank'=4] {'rank'}, use_global_device_ids=true, to_apply=%region_6.0 | all-reduce | flops 1024 | bytes 8192 | tf_op jit(solution)/shard_map/while/body/eval_jaxpr/psum | solution.py:19
  101.3 2.3 fusion.167
  104.2 1.6 fusion.164
  106.7 6.2 %psum.49 = f32[1024]{0:T(1024)S(1)} all-reduce(f32[1024]{0:T(1024)S(1)} %get-tuple-element.759), channel_id=1, replica_groups=mesh['blk'=8,'rank'=4] {'rank'}, use_global_device_ids=true, to_apply=%region_6.0 | all-reduce | flops 1024 | bytes 8192 | tf_op jit(solution)/shard_map/while/body/eval_jaxpr/psum | solution.py:19
  114.7 2.3 fusion.167
  117.0 3.2 %collective-permute-start.1 = (f32[64,1024]{1,0:T(8,128)S(1)}, f32[64,1024]{1,0:T(8,128)S(1)}, u32[]{:S(2)}, u32[]{:S(2)}) collective-permute-start(f32[64,1024]{1,0:T(8,128)S(1)} %get-tuple-element.505), channel_id=1, source_target_pairs={{28,0},{0,4},{4,8},{8,12},{12,16},{16,20},{20,24},{24,28},{29,1},{... | collective-permute-start | bytes 786440 | tf_op jit(solution)/shard_map/ppermute | solution.py:15
  120.2 5.1 %collective-permute-done.1 = f32[64,1024]{1,0:T(8,128)S(1)} collective-permute-done((f32[64,1024]{1,0:T(8,128)S(1)}, f32[64,1024]{1,0:T(8,128)S(1)}, u32[]{:S(2)}, u32[]{:S(2)}) %collective-permute-start.1) | collective-permute-done | bytes 262176 | tf_op jit(solution)/shard_map/ppermute | solution.py:15
  125.3 54.0 %while.62 = (s32[]{:T(128)}, f32[64,512]{1,0:T(8,128)S(1)}, f32[64,1024]{1,0:T(8,128)S(1)}, s32[]{:T(128)}, f32[4096]{0:T(1024)S(1)}, /*index=5*/s32[4096]{0:T(1...) while((s32[]{:T(128)}, f32[64,512]{1,0:T(8,128)S(1)}, ...), condition=%wide.region_11.0_spmd, body=%wide.region_8.0_spmd.sunk | while | flops 2419825664 | bytes 3092663 | solution.py:72
  128.5 5.7 %psum.50 = f32[1024]{0:T(1024)S(1)} all-reduce(f32[1024]{0:T(1024)S(1)} %get-tuple-element.768), channel_id=1, replica_groups=mesh['blk'=8,'rank'=4] {'rank'}, use_global_device_ids=true, to_apply=%region_10.0 | all-reduce | flops 1024 | bytes 8192 | tf_op jit(solution)/shard_map/while/body/eval_jaxpr/psum | solution.py:19
  136.1 2.3 fusion.175
  139.1 1.6 fusion.172
  141.7 6.2 %psum.50 = f32[1024]{0:T(1024)S(1)} all-reduce(f32[1024]{0:T(1024)S(1)} %get-tuple-element.768), channel_id=1, replica_groups=mesh['blk'=8,'rank'=4] {'rank'}, use_global_device_ids=true, to_apply=%region_10.0 | all-reduce | flops 1024 | bytes 8192 | tf_op jit(solution)/shard_map/while/body/eval_jaxpr/psum | solution.py:19
  149.8 2.3 fusion.175
  152.8 1.6 fusion.172
  155.4 5.7 %psum.50 = f32[1024]{0:T(1024)S(1)} all-reduce(f32[1024]{0:T(1024)S(1)} %get-tuple-element.768), channel_id=1, replica_groups=mesh['blk'=8,'rank'=4] {'rank'}, use_global_device_ids=true, to_apply=%region_10.0 | all-reduce | flops 1024 | bytes 8192 | tf_op jit(solution)/shard_map/while/body/eval_jaxpr/psum | solution.py:19
  162.9 2.3 fusion.175
  168.5 6.6 %psum.50 = f32[1024]{0:T(1024)S(1)} all-reduce(f32[1024]{0:T(1024)S(1)} %get-tuple-element.768), channel_id=1, replica_groups=mesh['blk'=8,'rank'=4] {'rank'}, use_global_device_ids=true, to_apply=%region_10.0 | all-reduce | flops 1024 | bytes 8192 | tf_op jit(solution)/shard_map/while/body/eval_jaxpr/psum | solution.py:19
  177.0 2.3 fusion.175
  179.3 5.2 %collective-permute-start.2 = (f32[64,1024]{1,0:T(8,128)S(1)}, f32[64,1024]{1,0:T(8,128)S(1)}, u32[]{:S(2)}, u32[]{:S(2)}) collective-permute-start(f32[64,1024]{1,0:T(8,128)S(1)} %get-tuple-element.507), channel_id=1, source_target_pairs={{28,0},{0,4},{4,8},{8,12},{12,16},{16,20},{20,24},{24,28},{29,1},{... | collective-permute-start | bytes 786440 | tf_op jit(solution)/shard_map/ppermute | solution.py:15
  184.5 4.7 %collective-permute-done.2 = f32[64,1024]{1,0:T(8,128)S(1)} collective-permute-done((f32[64,1024]{1,0:T(8,128)S(1)}, f32[64,1024]{1,0:T(8,128)S(1)}, u32[]{:S(2)}, u32[]{:S(2)}) %collective-permute-start.2) | collective-permute-done | bytes 262176 | tf_op jit(solution)/shard_map/ppermute | solution.py:15
  189.2 53.7 %while.63 = (s32[]{:T(128)}, f32[64,512]{1,0:T(8,128)S(1)}, f32[64,1024]{1,0:T(8,128)S(1)}, s32[]{:T(128)}, f32[4096]{0:T(1024)S(1)}, /*index=5*/s32[4096]{0:T(1...) while((s32[]{:T(128)}, f32[64,512]{1,0:T(8,128)S(1)}, ...), condition=%wide.region_15.0_spmd, body=%wide.region_12.0_spmd.sunk | while | flops 2419825664 | bytes 3092663 | solution.py:72
  192.4 5.7 %psum.51 = f32[1024]{0:T(1024)S(1)} all-reduce(f32[1024]{0:T(1024)S(1)} %get-tuple-element.777), channel_id=1, replica_groups=mesh['blk'=8,'rank'=4] {'rank'}, use_global_device_ids=true, to_apply=%region_14.0 | all-reduce | flops 1024 | bytes 8192 | tf_op jit(solution)/shard_map/while/body/eval_jaxpr/psum | solution.py:19
  199.9 2.3 fusion.183
  205.5 6.6 %psum.51 = f32[1024]{0:T(1024)S(1)} all-reduce(f32[1024]{0:T(1024)S(1)} %get-tuple-element.777), channel_id=1, replica_groups=mesh['blk'=8,'rank'=4] {'rank'}, use_global_device_ids=true, to_apply=%region_14.0 | all-reduce | flops 1024 | bytes 8192 | tf_op jit(solution)/shard_map/while/body/eval_jaxpr/psum | solution.py:19
  213.9 2.3 fusion.183
  217.0 1.6 fusion.180
  219.5 5.7 %psum.51 = f32[1024]{0:T(1024)S(1)} all-reduce(f32[1024]{0:T(1024)S(1)} %get-tuple-element.777), channel_id=1, replica_groups=mesh['blk'=8,'rank'=4] {'rank'}, use_global_device_ids=true, to_apply=%region_14.0 | all-reduce | flops 1024 | bytes 8192 | tf_op jit(solution)/shard_map/while/body/eval_jaxpr/psum | solution.py:19
  227.0 2.3 fusion.183
  232.5 6.2 %psum.51 = f32[1024]{0:T(1024)S(1)} all-reduce(f32[1024]{0:T(1024)S(1)} %get-tuple-element.777), channel_id=1, replica_groups=mesh['blk'=8,'rank'=4] {'rank'}, use_global_device_ids=true, to_apply=%region_14.0 | all-reduce | flops 1024 | bytes 8192 | tf_op jit(solution)/shard_map/while/body/eval_jaxpr/psum | solution.py:19
  240.6 2.3 fusion.183
  243.0 14.9 %collective-permute-done.3 = f32[64,1024]{1,0:T(8,128)S(1)} collective-permute-done((f32[64,1024]{1,0:T(8,128)S(1)}, f32[64,1024]{1,0:T(8,128)S(1)}, u32[]{:S(2)}, u32[]{:S(2)}) %collective-permute-start.3) | collective-permute-done | bytes 262176 | tf_op jit(solution)/shard_map/ppermute | solution.py:15
  (127 shorter events, 72.4 us)
Async XLA Ops:
  0.6 0.7 copy-start.6
  0.6 1.3 copy-start.3
  0.7 1.4 copy-start.4
  0.7 1.4 copy-start.5
  0.7 1.5 copy-start
  0.7 1.5 copy-start.2
  55.9 8.1 %collective-permute-start = (f32[64,1024]{1,0:T(8,128)S(1)}, f32[64,1024]{1,0:T(8,128)S(1)}, u32[]{:S(2)}, u32[]{:S(2)}) collective-permute-start(f32[64,1024]{1,0:T(8,128)S(1)} %get-tuple-element.503), channel_id=1, source_target_pairs={{28,0},{0,4},{4,8},{8,12},{12,16},{16,20},{20,24},{24,28},{29,1},{... | collective-permute-start | bytes 786440 | tf_op jit(solution)/shard_map/ppermute | solution.py:15
  117.0 8.3 %collective-permute-start.1 = (f32[64,1024]{1,0:T(8,128)S(1)}, f32[64,1024]{1,0:T(8,128)S(1)}, u32[]{:S(2)}, u32[]{:S(2)}) collective-permute-start(f32[64,1024]{1,0:T(8,128)S(1)} %get-tuple-element.505), channel_id=1, source_target_pairs={{28,0},{0,4},{4,8},{8,12},{12,16},{16,20},{20,24},{24,28},{29,1},{... | collective-permute-start | bytes 786440 | tf_op jit(solution)/shard_map/ppermute | solution.py:15
  179.3 9.9 %collective-permute-start.2 = (f32[64,1024]{1,0:T(8,128)S(1)}, f32[64,1024]{1,0:T(8,128)S(1)}, u32[]{:S(2)}, u32[]{:S(2)}) collective-permute-start(f32[64,1024]{1,0:T(8,128)S(1)} %get-tuple-element.507), channel_id=1, source_target_pairs={{28,0},{0,4},{4,8},{8,12},{12,16},{16,20},{20,24},{24,28},{29,1},{... | collective-permute-start | bytes 786440 | tf_op jit(solution)/shard_map/ppermute | solution.py:15
  242.9 15.7 %copy-start.1 = (f32[64,512]{1,0:T(8,128)}, f32[64,512]{1,0:T(8,128)S(1)}, u32[]{:S(2)}) copy-start(f32[64,512]{1,0:T(8,128)S(1)} %get-tuple-element.912) | copy-start | bytes 393220
  242.9 15.0 %collective-permute-start.3 = (f32[64,1024]{1,0:T(8,128)S(1)}, f32[64,1024]{1,0:T(8,128)S(1)}, u32[]{:S(2)}, u32[]{:S(2)}) collective-permute-start(f32[64,1024]{1,0:T(8,128)S(1)} %get-tuple-element.509), channel_id=1, source_target_pairs={{12,0},{16,4},{20,8},{24,12},{28,16},{0,20},{4,24},{8,28},{13,1},{... | collective-permute-start | bytes 786440 | tf_op jit(solution)/shard_map/ppermute | solution.py:15
where the time goes:
time: 259 us
  blocking collectives  96.6 us (37%)
  matrix products  96 us (37%)
  waiting for transfers between devices  32.7 us (13%)
  other arithmetic  20.4 us (8%)
  starting transfers between devices  8.61 us (3%)
    psum x16, blocking collectives, rank_total(): return lax.psum(partial_values, 'rank')  96.6 us
    dot_general x32, matrix products, spread_columns(): lax.dot_general(steps, chooser, (((1,), (1,)), ((), ())), preferred_eleme...  55.9 us
    dot_general x32, matrix products, pick_columns(): jnp.dot(block, chooser, preferred_element_type=jnp.float32, precision=lax...  40 us
    ppermute x4, waiting for transfers between devices, shifted(): return lax.ppermute(block, axis, route)  32.7 us
    mul x16, other arithmetic, update(): errors = weights * (targets - predicted)  10.2 us
    mul x16, other arithmetic, update(): DECAY_WEIGHT * weights[None, :] * user_vecs  10.2 us
    ppermute x4, starting transfers between devices, shifted(): return lax.ppermute(block, axis, route)  8.61 us
  transfers between devices with their start and end apart: 4, of which 4 were waited for; matrix products, arithmetic and copies ran while one was open for 0% of the time, Pallas kernels for 0%

commit v1 on v0

--- a/solution.py
+++ b/solution.py
@@ -16,7 +16,7 @@
 
 
 def rank_total(partial_values):
-    return lax.psum(partial_values, "rank")
+    return jnp.sum(lax.all_gather(partial_values, "rank"), axis=0)
 
 
 def selector(indices, count):

time: 259 us -> 250 us (0.965)
  blocking collectives: 96.6 us -> 83 us
  waiting for transfers between devices: 32.7 us -> 36.5 us
    psum x16 -> x0, blocking collectives: 96.6 us -> none  [rank_total(): return lax.psum(partial_values, 'rank')]
    all_gather x0 -> x16, blocking collectives: none -> 83 us  [rank_total(): return jnp.sum(lax.all_gather(partial_values, 'rank'), axis=0)]
    ppermute x4, waiting for transfers between devices: 32.7 us -> 36.5 us  [shifted(): return lax.ppermute(block, axis, route)]
where the time goes in v1:
time: 250 us; the launch traced here: 249 us
  matrix products  96 us (38%)
  blocking collectives  83 us (33%)
  waiting for transfers between devices  36.5 us (15%)
  other arithmetic  20.7 us (8%)
  starting transfers between devices  8.56 us (3%)
  local copies, waits for them, and re-layouts  2.6 us (1%)
    all_gather x16, blocking collectives, rank_total(): return jnp.sum(lax.all_gather(partial_values, 'rank'), axis=0)  83 us
    dot_general x32, matrix products, spread_columns(): lax.dot_general(steps, chooser, (((1,), (1,)), ((), ())), preferred_eleme...  56 us
    dot_general x32, matrix products, pick_columns(): jnp.dot(block, chooser, preferred_element_type=jnp.float32, precision=lax...  40 us
    ppermute x4, waiting for transfers between devices, shifted(): return lax.ppermute(block, axis, route)  36.5 us
    mul x16, other arithmetic, update(): errors = weights * (targets - predicted)  10.2 us
    mul x16, other arithmetic, update(): DECAY_WEIGHT * weights[None, :] * user_vecs  10.2 us
    ppermute x4, starting transfers between devices, shifted(): return lax.ppermute(block, axis, route)  8.56 us
  transfers between devices with their start and end apart: 4, of which 4 were waited for; matrix products, arithmetic and copies ran while one was open for 0% of the time, Pallas kernels for 0%

profile of v1, /device:TPU:28, one launch (start us, length us, event | category | flops | bytes accessed | tf_op | source)
XLA Modules:
  0.0 249.3 jit_solution(2055894451000102115)
XLA Ops:
  2.2 50.4 %while.60 = (s32[]{:T(128)}, f32[64,512]{1,0:T(8,128)S(1)}, f32[64,1024]{1,0:T(8,128)S(1)}, s32[]{:T(128)}, f32[4096]{0:T(1024)S(1)}, /*index=5*/s32[4096]{0:T(1...) while((s32[]{:T(128)}, f32[64,512]{1,0:T(8,128)S(1)}, ...), condition=%wide.region_3.0_spmd, body=%wide.region_0.0_spmd.sunk | while | flops 2419827712 | bytes 3158211 | solution.py:72
  5.4 5.2 %all-gather.8 = f32[4096]{0:T(1024)S(1)} all-gather(f32[1024]{0:T(1024)S(1)} %get-tuple-element.750), channel_id=2, replica_groups=mesh['blk'=8,'rank'=4] {'rank'}, dimensions={0}, use_global_device_ids=true | all-gather | bytes 20480 | tf_op jit(solution)/shard_map/while/body/eval_jaxpr/all_gather | solution.py:19
  12.4 2.3 fusion.159
  18.0 5.2 %all-gather.8 = f32[4096]{0:T(1024)S(1)} all-gather(f32[1024]{0:T(1024)S(1)} %get-tuple-element.750), channel_id=2, replica_groups=mesh['blk'=8,'rank'=4] {'rank'}, dimensions={0}, use_global_device_ids=true | all-gather | bytes 20480 | tf_op jit(solution)/shard_map/while/body/eval_jaxpr/all_gather | solution.py:19
  25.0 2.3 fusion.159
  30.5 5.2 %all-gather.8 = f32[4096]{0:T(1024)S(1)} all-gather(f32[1024]{0:T(1024)S(1)} %get-tuple-element.750), channel_id=2, replica_groups=mesh['blk'=8,'rank'=4] {'rank'}, dimensions={0}, use_global_device_ids=true | all-gather | bytes 20480 | tf_op jit(solution)/shard_map/while/body/eval_jaxpr/all_gather | solution.py:19
  37.6 2.3 fusion.159
  43.1 5.2 %all-gather.8 = f32[4096]{0:T(1024)S(1)} all-gather(f32[1024]{0:T(1024)S(1)} %get-tuple-element.750), channel_id=2, replica_groups=mesh['blk'=8,'rank'=4] {'rank'}, dimensions={0}, use_global_device_ids=true | all-gather | bytes 20480 | tf_op jit(solution)/shard_map/while/body/eval_jaxpr/all_gather | solution.py:19
  50.2 2.3 fusion.159
  52.6 8.5 %collective-permute-done = f32[64,1024]{1,0:T(8,128)S(1)} collective-permute-done((f32[64,1024]{1,0:T(8,128)S(1)}, f32[64,1024]{1,0:T(8,128)S(1)}, u32[]{:S(2)}, u32[]{:S(2)}) %collective-permute-start) | collective-permute-done | bytes 262176 | tf_op jit(solution)/shard_map/ppermute | solution.py:15
  61.1 49.7 %while.61 = (s32[]{:T(128)}, f32[64,512]{1,0:T(8,128)S(1)}, f32[64,1024]{1,0:T(8,128)S(1)}, s32[]{:T(128)}, f32[4096]{0:T(1024)S(1)}, /*index=5*/s32[4096]{0:T(1...) while((s32[]{:T(128)}, f32[64,512]{1,0:T(8,128)S(1)}, ...), condition=%wide.region_7.0_spmd, body=%wide.region_4.0_spmd.sunk | while | flops 2419827712 | bytes 3158211 | solution.py:72
  61.7 1.6 fusion.164
  64.2 5.2 %all-gather.9 = f32[4096]{0:T(1024)S(1)} all-gather(f32[1024]{0:T(1024)S(1)} %get-tuple-element.759), channel_id=3, replica_groups=mesh['blk'=8,'rank'=4] {'rank'}, dimensions={0}, use_global_device_ids=true | all-gather | bytes 20480 | tf_op jit(solution)/shard_map/while/body/eval_jaxpr/all_gather | solution.py:19
  71.2 2.3 fusion.167
  74.1 1.6 fusion.164
  76.6 5.2 %all-gather.9 = f32[4096]{0:T(1024)S(1)} all-gather(f32[1024]{0:T(1024)S(1)} %get-tuple-element.759), channel_id=3, replica_groups=mesh['blk'=8,'rank'=4] {'rank'}, dimensions={0}, use_global_device_ids=true | all-gather | bytes 20480 | tf_op jit(solution)/shard_map/while/body/eval_jaxpr/all_gather | solution.py:19
  83.6 2.3 fusion.167
  86.6 1.6 fusion.164
  89.1 5.2 %all-gather.9 = f32[4096]{0:T(1024)S(1)} all-gather(f32[1024]{0:T(1024)S(1)} %get-tuple-element.759), channel_id=3, replica_groups=mesh['blk'=8,'rank'=4] {'rank'}, dimensions={0}, use_global_device_ids=true | all-gather | bytes 20480 | tf_op jit(solution)/shard_map/while/body/eval_jaxpr/all_gather | solution.py:19
  96.1 2.3 fusion.167
  99.0 1.6 fusion.164
  101.5 5.2 %all-gather.9 = f32[4096]{0:T(1024)S(1)} all-gather(f32[1024]{0:T(1024)S(1)} %get-tuple-element.759), channel_id=3, replica_groups=mesh['blk'=8,'rank'=4] {'rank'}, dimensions={0}, use_global_device_ids=true | all-gather | bytes 20480 | tf_op jit(solution)/shard_map/while/body/eval_jaxpr/all_gather | solution.py:19
  108.5 2.3 fusion.167
  110.8 3.2 %collective-permute-start.1 = (f32[64,1024]{1,0:T(8,128)S(1)}, f32[64,1024]{1,0:T(8,128)S(1)}, u32[]{:S(2)}, u32[]{:S(2)}) collective-permute-start(f32[64,1024]{1,0:T(8,128)S(1)} %get-tuple-element.505), channel_id=1, source_target_pairs={{28,0},{0,4},{4,8},{8,12},{12,16},{16,20},{20,24},{24,28},{29,1},{... | collective-permute-start | bytes 786440 | tf_op jit(solution)/shard_map/ppermute | solution.py:15
  114.0 6.0 %collective-permute-done.1 = f32[64,1024]{1,0:T(8,128)S(1)} collective-permute-done((f32[64,1024]{1,0:T(8,128)S(1)}, f32[64,1024]{1,0:T(8,128)S(1)}, u32[]{:S(2)}, u32[]{:S(2)}) %collective-permute-start.1) | collective-permute-done | bytes 262176 | tf_op jit(solution)/shard_map/ppermute | solution.py:15
  120.1 50.8 %while.62 = (s32[]{:T(128)}, f32[64,512]{1,0:T(8,128)S(1)}, f32[64,1024]{1,0:T(8,128)S(1)}, s32[]{:T(128)}, f32[4096]{0:T(1024)S(1)}, /*index=5*/s32[4096]{0:T(1...) while((s32[]{:T(128)}, f32[64,512]{1,0:T(8,128)S(1)}, ...), condition=%wide.region_11.0_spmd, body=%wide.region_8.0_spmd.sunk | while | flops 2419827712 | bytes 3158211 | solution.py:72
  123.3 5.2 %all-gather.10 = f32[4096]{0:T(1024)S(1)} all-gather(f32[1024]{0:T(1024)S(1)} %get-tuple-element.768), channel_id=4, replica_groups=mesh['blk'=8,'rank'=4] {'rank'}, dimensions={0}, use_global_device_ids=true | all-gather | bytes 20480 | tf_op jit(solution)/shard_map/while/body/eval_jaxpr/all_gather | solution.py:19
  130.4 2.3 fusion.175
  133.5 1.6 fusion.172
  136.0 5.2 %all-gather.10 = f32[4096]{0:T(1024)S(1)} all-gather(f32[1024]{0:T(1024)S(1)} %get-tuple-element.768), channel_id=4, replica_groups=mesh['blk'=8,'rank'=4] {'rank'}, dimensions={0}, use_global_device_ids=true | all-gather | bytes 20480 | tf_op jit(solution)/shard_map/while/body/eval_jaxpr/all_gather | solution.py:19
  143.1 2.3 fusion.175
  146.2 1.6 fusion.172
  148.7 5.2 %all-gather.10 = f32[4096]{0:T(1024)S(1)} all-gather(f32[1024]{0:T(1024)S(1)} %get-tuple-element.768), channel_id=4, replica_groups=mesh['blk'=8,'rank'=4] {'rank'}, dimensions={0}, use_global_device_ids=true | all-gather | bytes 20480 | tf_op jit(solution)/shard_map/while/body/eval_jaxpr/all_gather | solution.py:19
  155.8 2.3 fusion.175
  161.4 5.2 %all-gather.10 = f32[4096]{0:T(1024)S(1)} all-gather(f32[1024]{0:T(1024)S(1)} %get-tuple-element.768), channel_id=4, replica_groups=mesh['blk'=8,'rank'=4] {'rank'}, dimensions={0}, use_global_device_ids=true | all-gather | bytes 20480 | tf_op jit(solution)/shard_map/while/body/eval_jaxpr/all_gather | solution.py:19
  168.5 2.3 fusion.175
  170.9 5.2 %collective-permute-start.2 = (f32[64,1024]{1,0:T(8,128)S(1)}, f32[64,1024]{1,0:T(8,128)S(1)}, u32[]{:S(2)}, u32[]{:S(2)}) collective-permute-start(f32[64,1024]{1,0:T(8,128)S(1)} %get-tuple-element.507), channel_id=1, source_target_pairs={{28,0},{0,4},{4,8},{8,12},{12,16},{16,20},{20,24},{24,28},{29,1},{... | collective-permute-start | bytes 786440 | tf_op jit(solution)/shard_map/ppermute | solution.py:15
  176.1 6.0 %collective-permute-done.2 = f32[64,1024]{1,0:T(8,128)S(1)} collective-permute-done((f32[64,1024]{1,0:T(8,128)S(1)}, f32[64,1024]{1,0:T(8,128)S(1)}, u32[]{:S(2)}, u32[]{:S(2)}) %collective-permute-start.2) | collective-permute-done | bytes 262176 | tf_op jit(solution)/shard_map/ppermute | solution.py:15
  182.1 50.4 %while.63 = (s32[]{:T(128)}, f32[64,512]{1,0:T(8,128)S(1)}, f32[64,1024]{1,0:T(8,128)S(1)}, s32[]{:T(128)}, f32[4096]{0:T(1024)S(1)}, /*index=5*/s32[4096]{0:T(1...) while((s32[]{:T(128)}, f32[64,512]{1,0:T(8,128)S(1)}, ...), condition=%wide.region_15.0_spmd, body=%wide.region_12.0_spmd.sunk | while | flops 2419827712 | bytes 3158211 | solution.py:72
  185.3 5.2 %all-gather.11 = f32[4096]{0:T(1024)S(1)} all-gather(f32[1024]{0:T(1024)S(1)} %get-tuple-element.777), channel_id=5, replica_groups=mesh['blk'=8,'rank'=4] {'rank'}, dimensions={0}, use_global_device_ids=true | all-gather | bytes 20480 | tf_op jit(solution)/shard_map/while/body/eval_jaxpr/all_gather | solution.py:19
  192.4 2.3 fusion.183
  197.9 5.2 %all-gather.11 = f32[4096]{0:T(1024)S(1)} all-gather(f32[1024]{0:T(1024)S(1)} %get-tuple-element.777), channel_id=5, replica_groups=mesh['blk'=8,'rank'=4] {'rank'}, dimensions={0}, use_global_device_ids=true | all-gather | bytes 20480 | tf_op jit(solution)/shard_map/while/body/eval_jaxpr/all_gather | solution.py:19
  205.0 2.3 fusion.183
  210.5 5.2 %all-gather.11 = f32[4096]{0:T(1024)S(1)} all-gather(f32[1024]{0:T(1024)S(1)} %get-tuple-element.777), channel_id=5, replica_groups=mesh['blk'=8,'rank'=4] {'rank'}, dimensions={0}, use_global_device_ids=true | all-gather | bytes 20480 | tf_op jit(solution)/shard_map/while/body/eval_jaxpr/all_gather | solution.py:19
  217.6 2.3 fusion.183
  223.2 5.2 %all-gather.11 = f32[4096]{0:T(1024)S(1)} all-gather(f32[1024]{0:T(1024)S(1)} %get-tuple-element.777), channel_id=5, replica_groups=mesh['blk'=8,'rank'=4] {'rank'}, dimensions={0}, use_global_device_ids=true | all-gather | bytes 20480 | tf_op jit(solution)/shard_map/while/body/eval_jaxpr/all_gather | solution.py:19
  230.2 2.3 fusion.183
  232.6 15.9 %collective-permute-done.3 = f32[64,1024]{1,0:T(8,128)S(1)} collective-permute-done((f32[64,1024]{1,0:T(8,128)S(1)}, f32[64,1024]{1,0:T(8,128)S(1)}, u32[]{:S(2)}, u32[]{:S(2)}) %collective-permute-start.3) | collective-permute-done | bytes 262176 | tf_op jit(solution)/shard_map/ppermute | solution.py:15
  (159 shorter events, 72.8 us)
Async XLA Ops:
  0.6 0.7 copy-start.6
  0.6 1.3 copy-start.3
  0.7 1.4 copy-start.4
  0.7 1.4 copy-start.5
  0.7 1.5 copy-start
  0.7 1.5 copy-start.2
  52.5 8.6 %collective-permute-start = (f32[64,1024]{1,0:T(8,128)S(1)}, f32[64,1024]{1,0:T(8,128)S(1)}, u32[]{:S(2)}, u32[]{:S(2)}) collective-permute-start(f32[64,1024]{1,0:T(8,128)S(1)} %get-tuple-element.503), channel_id=1, source_target_pairs={{28,0},{0,4},{4,8},{8,12},{12,16},{16,20},{20,24},{24,28},{29,1},{... | collective-permute-start | bytes 786440 | tf_op jit(solution)/shard_map/ppermute | solution.py:15
  110.8 9.2 %collective-permute-start.1 = (f32[64,1024]{1,0:T(8,128)S(1)}, f32[64,1024]{1,0:T(8,128)S(1)}, u32[]{:S(2)}, u32[]{:S(2)}) collective-permute-start(f32[64,1024]{1,0:T(8,128)S(1)} %get-tuple-element.505), channel_id=1, source_target_pairs={{28,0},{0,4},{4,8},{8,12},{12,16},{16,20},{20,24},{24,28},{29,1},{... | collective-permute-start | bytes 786440 | tf_op jit(solution)/shard_map/ppermute | solution.py:15
  170.9 11.3 %collective-permute-start.2 = (f32[64,1024]{1,0:T(8,128)S(1)}, f32[64,1024]{1,0:T(8,128)S(1)}, u32[]{:S(2)}, u32[]{:S(2)}) collective-permute-start(f32[64,1024]{1,0:T(8,128)S(1)} %get-tuple-element.507), channel_id=1, source_target_pairs={{28,0},{0,4},{4,8},{8,12},{12,16},{16,20},{20,24},{24,28},{29,1},{... | collective-permute-start | bytes 786440 | tf_op jit(solution)/shard_map/ppermute | solution.py:15
  232.6 16.7 %copy-start.1 = (f32[64,512]{1,0:T(8,128)}, f32[64,512]{1,0:T(8,128)S(1)}, u32[]{:S(2)}) copy-start(f32[64,512]{1,0:T(8,128)S(1)} %get-tuple-element.924) | copy-start | bytes 393220
  232.6 16.0 %collective-permute-start.3 = (f32[64,1024]{1,0:T(8,128)S(1)}, f32[64,1024]{1,0:T(8,128)S(1)}, u32[]{:S(2)}, u32[]{:S(2)}) collective-permute-start(f32[64,1024]{1,0:T(8,128)S(1)} %get-tuple-element.509), channel_id=1, source_target_pairs={{12,0},{16,4},{20,8},{24,12},{28,16},{0,20},{4,24},{8,28},{13,1},{... | collective-permute-start | bytes 786440 | tf_op jit(solution)/shard_map/ppermute | solution.py:15
